TPU v7x, 32 devices: a whole 2x2x4 slice. The times are simulated.
32 devices in a mesh: dp: 8 (over z, x), tensor: 4 (over y, core).
Axes of the slice: x: 2, y: 2, z: 4, core: 2. Of those that a mesh axis runs over, the one named last changes fastest.
Arguments:
- tokens: bfloat16 [8192, 640], P(('dp', 'tensor')), may hold values from -6 to 6
- segments: int32 [8192], P(('dp', 'tensor')), may hold values from 0 to 31, as said below
- query_weight: bfloat16 [640, 1024], P('dp', 'tensor'), may hold values from -0.25 to 0.25
- keyvalue_weight: bfloat16 [640, 512], P('dp'), may hold values from -0.25 to 0.25
- output_weight: bfloat16 [1024, 640], P('tensor', 'dp'), may hold values from -0.1875 to 0.1875
- gate_weight: bfloat16 [640, 2048], P('dp', 'tensor'), may hold values from -0.25 to 0.25
- up_weight: bfloat16 [640, 2048], P('dp', 'tensor'), may hold values from -0.25 to 0.25
- down_weight: bfloat16 [2048, 640], P('tensor', 'dp'), may hold values from -0.125 to 0.125
- norm_gains: float32 [4, 640], replicated, may hold values from 0.5 to 1.5
- headnorm_gains: float32 [2, 256], replicated, may hold values from 0.5 to 1.5
- cotangent: bfloat16 [8192, 640], P(('dp', 'tensor')), may hold values from -6 to 6
Outputs:
- output: bfloat16 [8192, 640], P(('dp', 'tensor'))
- grad_tokens: float32 [8192, 640], P(('dp', 'tensor'))
- grad_query_weight: float32 [640, 1024], P('dp', 'tensor')
- grad_keyvalue_weight: float32 [640, 512], P('dp', 'tensor')
- grad_output_weight: float32 [1024, 640], P('tensor', 'dp')
- grad_gate_weight: float32 [640, 2048], P('dp', 'tensor')
- grad_up_weight: float32 [640, 2048], P('dp', 'tensor')
- grad_down_weight: float32 [2048, 640], P('tensor', 'dp')
- grad_norm_gains: float32 [4, 640], P('tensor', 'dp')
- grad_headnorm_gains: float32 [2, 256], P(None, ('dp', 'tensor'))
Inputs may be any that keep to these rules, and one draw needn't show every extreme that they name: `segments`: sequence s (tokens s * 1024 to (s + 1) * 1024 - 1) holds exactly four documents in order, numbered 4 s to 4 s + 3; the second begins before position 256 and ends after position 768 of its sequence.
All inputs are finite; a program needn't handle non-finite values.
Results may differ from a plain program's by a relative error of at most 0.024.
Values may be sent and summed in bfloat16 or wider, within the bound.
A program may use at most 128 MiB of HBM per device.

v0:
```python
import jax
import jax.numpy as jnp
from jax import lax
from jax.sharding import PartitionSpec as P

epsilon = 1e-06
rope_base = 1000000.0
score_scale = 0.0625


def norm_rows(values, scaling):
    return values * lax.rsqrt(jnp.mean(values * values, axis=-1, keepdims=True) + epsilon) * scaling


def angles(length, head_width):
    halfway = head_width // 2
    places = jnp.arange(length, dtype=jnp.float32)[:, None]
    frequency = rope_base ** (-2.0 * jnp.arange(halfway, dtype=jnp.float32) / head_width)
    phases = places * frequency[None, :]
    return (jnp.cos(phases), jnp.sin(phases))


def rotate(values, cosine_table, sine_table):
    halfway = values.shape[-1] // 2
    leading = values[..., :halfway]
    trailing = values[..., halfway:]
    return jnp.concatenate(
        [
            leading * cosine_table - trailing * sine_table,
            trailing * cosine_table + leading * sine_table,
        ],
        axis=-1,
    )


def activate(gating, upward):
    return jax.nn.gelu(gating, approximate=True) * upward


def dot_rows(left_side, right_side):
    return jnp.dot(left_side, right_side, preferred_element_type=jnp.float32)


def dot_inner(left_side, right_side):
    return lax.dot_general(
        left_side, right_side, (((1,), (1,)), ((), ())), preferred_element_type=jnp.float32
    )


def dot_outer(left_side, right_side):
    return lax.dot_general(
        left_side, right_side, (((0,), (0,)), ((), ())), preferred_element_type=jnp.float32
    )


def spread_blocks(whole, row_groups, column_groups):
    height = whole.shape[0] // row_groups
    breadth = whole.shape[1] // column_groups
    blocks = whole.reshape(row_groups, height, column_groups, breadth).transpose(0, 2, 1, 3)
    return blocks.reshape(row_groups * column_groups, height * breadth)


def body(
    tokens,
    segments,
    query_weight,
    keyvalue_weight,
    output_weight,
    gate_weight,
    up_weight,
    down_weight,
    norm_gains,
    headnorm_gains,
    cotangent,
):
    head_width = headnorm_gains.shape[1]
    dp_count = lax.axis_size("dp")
    tensor_count = lax.axis_size("tensor")
    inputs = tokens.astype(jnp.float32)
    first_normed = norm_rows(inputs, norm_gains[0]).astype(jnp.bfloat16)
    rows_all, segment_all = (
        lax.all_gather(first_normed, "tensor", axis=0, tiled=True),
        lax.all_gather(segments, "tensor", axis=0, tiled=True),
    )
    query_full, keyvalue_full, output_full = (
        lax.all_gather(query_weight, "dp", axis=0, tiled=True),
        lax.all_gather(keyvalue_weight, "dp", axis=0, tiled=True),
        lax.all_gather(output_weight, "dp", axis=1, tiled=True),
    )
    length = rows_all.shape[0]
    block_rows = min(512, length)
    cosine_table, sine_table = angles(length, head_width)

    def query_map(raw_values, scaling):
        return rotate(norm_rows(raw_values, scaling), cosine_table, sine_table) * score_scale

    def key_map(raw_values, scaling):
        return rotate(norm_rows(raw_values, scaling), cosine_table, sine_table)

    query_raw = dot_rows(rows_all, query_full)
    keyvalue_raw = dot_rows(rows_all, keyvalue_full)
    query_rows = query_map(query_raw, headnorm_gains[0]).astype(jnp.bfloat16)
    key_rows = key_map(keyvalue_raw[:, :head_width], headnorm_gains[1]).astype(jnp.bfloat16)
    value_rows = keyvalue_raw[:, head_width:].astype(jnp.bfloat16)

    def masked_scores(row_from, row_to):
        scores = dot_inner(query_rows[row_from:row_to], key_rows[:row_to])
        row_places = row_from + jnp.arange(row_to - row_from)
        key_places = jnp.arange(row_to)
        allowed = (key_places[None, :] <= row_places[:, None]) & (
            segment_all[row_from:row_to][:, None] == segment_all[:row_to][None, :]
        )
        return jnp.where(allowed, scores, -jnp.inf)

    pieces_out = []
    pieces_total = []
    for block_id in range(length // block_rows):
        row_from = block_id * block_rows
        row_to = row_from + block_rows
        scores = masked_scores(row_from, row_to)
        row_peak = jnp.max(scores, axis=-1, keepdims=True)
        raised = jnp.exp(scores - row_peak)
        row_total = jnp.sum(raised, axis=-1, keepdims=True)
        weights_low = (raised / row_total).astype(jnp.bfloat16)
        pieces_out.append(dot_rows(weights_low, value_rows[:row_to]).astype(jnp.bfloat16))
        pieces_total.append(row_peak + jnp.log(row_total))
    attended = jnp.concatenate(pieces_out, axis=0)
    log_totals = jnp.concatenate(pieces_total, axis=0)
    branch = lax.psum_scatter(
        dot_rows(attended, output_full), "tensor", scatter_dimension=0, tiled=True
    )
    middle = inputs + norm_rows(branch, norm_gains[1])
    mid_normed = norm_rows(middle, norm_gains[2]).astype(jnp.bfloat16)
    mid_all = lax.all_gather(mid_normed, "tensor", axis=0, tiled=True)
    gate_full, up_full, down_full = (
        lax.all_gather(gate_weight, "dp", axis=0, tiled=True),
        lax.all_gather(up_weight, "dp", axis=0, tiled=True),
        lax.all_gather(down_weight, "dp", axis=1, tiled=True),
    )
    gating = dot_rows(mid_all, gate_full)
    upward = dot_rows(mid_all, up_full)
    hidden = activate(gating, upward).astype(jnp.bfloat16)
    ffn_out = lax.psum_scatter(
        dot_rows(hidden, down_full).astype(jnp.bfloat16), "tensor", scatter_dimension=0, tiled=True
    ).astype(jnp.float32)
    outcome = (middle + norm_rows(ffn_out, norm_gains[3])).astype(jnp.bfloat16)
    upstream = cotangent.astype(jnp.float32)
    ignored, pull_last = jax.vjp(norm_rows, ffn_out, norm_gains[3])
    grad_ffn, gain_last = pull_last(upstream)
    grad_ffn_all = lax.all_gather(grad_ffn.astype(jnp.bfloat16), "tensor", axis=0, tiled=True)
    grad_hidden = dot_inner(grad_ffn_all, down_full)
    down_grad = dot_outer(hidden, grad_ffn_all)
    ignored, pull_active = jax.vjp(activate, gating, upward)
    grad_gating, grad_upward = pull_active(grad_hidden)
    gating_low = grad_gating.astype(jnp.bfloat16)
    upward_low = grad_upward.astype(jnp.bfloat16)
    gate_grad = dot_outer(mid_all, gating_low)
    up_grad = dot_outer(mid_all, upward_low)
    grad_mid_normed = lax.psum_scatter(
        (dot_inner(gating_low, gate_full) + dot_inner(upward_low, up_full)).astype(jnp.bfloat16),
        "tensor",
        scatter_dimension=0,
        tiled=True,
    ).astype(jnp.float32)
    gate_part, up_part, down_part = (
        lax.psum_scatter(gate_grad, "dp", scatter_dimension=0, tiled=True),
        lax.psum_scatter(up_grad, "dp", scatter_dimension=0, tiled=True),
        lax.psum_scatter(down_grad, "dp", scatter_dimension=1, tiled=True),
    )
    ignored, pull_mid = jax.vjp(norm_rows, middle, norm_gains[2])
    grad_middle_part, gain_mid = pull_mid(grad_mid_normed)
    grad_middle = upstream + grad_middle_part
    ignored, pull_branch = jax.vjp(norm_rows, branch, norm_gains[1])
    grad_branch, gain_branch = pull_branch(grad_middle)
    branch_all = lax.all_gather(grad_branch.astype(jnp.bfloat16), "tensor", axis=0, tiled=True)
    output_grad = dot_outer(attended, branch_all)
    grad_attended = dot_inner(branch_all, output_full).astype(jnp.bfloat16)
    grad_query_parts = []
    grad_keys = jnp.zeros((length, head_width), jnp.float32)
    grad_values = jnp.zeros((length, head_width), jnp.float32)
    for block_id in range(length // block_rows):
        row_from = block_id * block_rows
        row_to = row_from + block_rows
        scores = masked_scores(row_from, row_to)
        weights_full = jnp.exp(scores - log_totals[row_from:row_to])
        weights_low = weights_full.astype(jnp.bfloat16)
        grad_block = grad_attended[row_from:row_to]
        grad_weights = dot_inner(grad_block, value_rows[:row_to])
        row_inner = jnp.sum(weights_full * grad_weights, axis=-1, keepdims=True)
        grad_scores = (weights_full * (grad_weights - row_inner)).astype(jnp.bfloat16)
        grad_query_parts.append(dot_rows(grad_scores, key_rows[:row_to]))
        grad_keys = grad_keys.at[:row_to].add(dot_outer(grad_scores, query_rows[row_from:row_to]))
        grad_values = grad_values.at[:row_to].add(dot_outer(weights_low, grad_block))
    grad_query = jnp.concatenate(grad_query_parts, axis=0)
    ignored, pull_query = jax.vjp(query_map, query_raw, headnorm_gains[0])
    grad_query_raw, gain_query = pull_query(grad_query)
    ignored, pull_key = jax.vjp(key_map, keyvalue_raw[:, :head_width], headnorm_gains[1])
    grad_key_raw, gain_key = pull_key(grad_keys)
    query_grad_low = grad_query_raw.astype(jnp.bfloat16)
    keyvalue_grad_low = jnp.concatenate([grad_key_raw, grad_values], axis=1).astype(jnp.bfloat16)
    query_grad = dot_outer(rows_all, query_grad_low)
    keyvalue_grad = dot_outer(rows_all, keyvalue_grad_low)
    grad_first_normed = lax.psum_scatter(
        (
            dot_inner(query_grad_low, query_full) + dot_inner(keyvalue_grad_low, keyvalue_full)
        ).astype(jnp.bfloat16),
        "tensor",
        scatter_dimension=0,
        tiled=True,
    ).astype(jnp.float32)
    ignored, pull_first = jax.vjp(norm_rows, inputs, norm_gains[0])
    grad_inputs, gain_first = pull_first(grad_first_normed)
    grad_tokens = grad_middle + grad_inputs
    query_part, output_part = (
        lax.psum_scatter(query_grad, "dp", scatter_dimension=0, tiled=True),
        lax.psum_scatter(output_grad, "dp", scatter_dimension=1, tiled=True),
    )
    gain_stack = jnp.stack([gain_first, gain_branch, gain_mid, gain_last], axis=0)
    headgain_stack = jnp.stack([gain_query, gain_key], axis=0)
    keyvalue_flat = spread_blocks(keyvalue_grad, dp_count, tensor_count)
    gains_flat = spread_blocks(gain_stack.T, dp_count, tensor_count)
    headgains_flat = spread_blocks(headgain_stack.T, dp_count * tensor_count, 1)
    keyvalue_part, gains_part, headgains_part = (
        lax.psum_scatter(keyvalue_flat, ("dp", "tensor"), scatter_dimension=0, tiled=True),
        lax.psum_scatter(gains_flat, ("dp", "tensor"), scatter_dimension=0, tiled=True),
        lax.psum_scatter(headgains_flat, ("dp", "tensor"), scatter_dimension=0, tiled=True),
    )
    keyvalue_part = keyvalue_part.reshape(
        keyvalue_weight.shape[0], keyvalue_weight.shape[1] // tensor_count
    )
    gains_part = gains_part.reshape(
        norm_gains.shape[1] // dp_count, norm_gains.shape[0] // tensor_count
    ).T
    headgains_part = headgains_part.reshape(head_width // (dp_count * tensor_count), 2).T
    return (
        outcome,
        grad_tokens,
        query_part,
        keyvalue_part,
        output_part,
        gate_part,
        up_part,
        down_part,
        gains_part,
        headgains_part,
    )


def solution(mesh):
    placed = (
        P(("dp", "tensor"), None),
        P(("dp", "tensor")),
        P("dp", "tensor"),
        P("dp", None),
        P("tensor", "dp"),
        P("dp", "tensor"),
        P("dp", "tensor"),
        P("tensor", "dp"),
        P(),
        P(),
        P(("dp", "tensor"), None),
    )
    return jax.shard_map(
        body,
        mesh=mesh,
        in_specs=placed,
        out_specs=(
            P(("dp", "tensor"), None),
            P(("dp", "tensor"), None),
            P("dp", "tensor"),
            P("dp", "tensor"),
            P("tensor", "dp"),
            P("dp", "tensor"),
            P("dp", "tensor"),
            P("tensor", "dp"),
            P("tensor", "dp"),
            P(None, ("dp", "tensor")),
        ),
        check_vma=False,
    )
```

profile of v0, /device:TPU:0, one launch (start us, length us, event | category | flops | bytes accessed | tf_op | source)
XLA Modules:
  0.0 910.7 jit_solution(9286828777555048314)
XLA Ops:
  12.3 6.3 all-gather
  18.6 32.0 %all_gather.35 = bf16[640,256]{1,0:T(8,128)(2,1)S(1)} all-gather(bf16[80,256]{1,0:T(8,128)(2,1)} %param.25), channel_id=1, replica_groups=mesh['dp'=8,'tensor'=4] {'dp'}, dimensions={0}, use_global_device_ids=true | all-gather | bytes 368640 | tf_op jit(solution)/shard_map/all_gather | solution.py:86
  50.6 33.1 %all_gather.37 = bf16[256,640]{0,1:T(8,128)(2,1)} all-gather(bf16[256,80]{0,1:T(8,128)(2,1)} %param.27), channel_id=1, replica_groups=mesh['dp'=8,'tensor'=4] {'dp'}, dimensions={1}, use_global_device_ids=true | all-gather | bytes 368640 | tf_op jit(solution)/shard_map/all_gather | solution.py:88
  83.8 31.6 %all_gather.36 = bf16[640,512]{1,0:T(8,128)(2,1)S(1)} all-gather(bf16[80,512]{1,0:T(8,128)(2,1)S(1)} %copy-done.43), channel_id=1, replica_groups=mesh['dp'=8,'tensor'=4] {'dp'}, dimensions={0}, use_global_device_ids=true | all-gather | bytes 737280 | tf_op jit(solution)/shard_map/all_gather | solution.py:87
  115.4 2.2 multiply_reduce_fusion.7
  120.1 2.4 multiply_subtract_fusion
  128.5 35.9 %reduce-scatter.10.cloned.1.call-done = f32[256,640]{1,0:T(8,128)} async-done(((f32[1024,640]{1,0:T(8,128)}), f32[256,640]{1,0:T(8,128)}) %reduce-scatter.10.cloned.1.call-update) | async-done | bytes 655376 | tf_op jit(solution)/shard_map/reduce_scatter | solution.py:129
  170.2 34.0 %all_gather.39 = bf16[640,512]{1,0:T(8,128)(2,1)} all-gather(bf16[80,512]{1,0:T(8,128)(2,1)S(1)} %copy-done.44), channel_id=1, replica_groups=mesh['dp'=8,'tensor'=4] {'dp'}, dimensions={0}, use_global_device_ids=true | all-gather | bytes 737280 | tf_op jit(solution)/shard_map/all_gather | solution.py:136
  204.2 34.1 %all_gather.40 = bf16[640,512]{1,0:T(8,128)(2,1)} all-gather(bf16[80,512]{1,0:T(8,128)(2,1)} %param.29), channel_id=1, replica_groups=mesh['dp'=8,'tensor'=4] {'dp'}, dimensions={0}, use_global_device_ids=true | all-gather | bytes 737280 | tf_op jit(solution)/shard_map/all_gather | solution.py:137
  238.3 34.1 %all_gather.41 = bf16[512,640]{0,1:T(8,128)(2,1)} all-gather(bf16[512,80]{0,1:T(8,128)(2,1)} %param.30), channel_id=1, replica_groups=mesh['dp'=8,'tensor'=4] {'dp'}, dimensions={1}, use_global_device_ids=true | all-gather | bytes 737280 | tf_op jit(solution)/shard_map/all_gather | solution.py:138
  272.4 2.6 fusion.86
  275.1 2.6 multiply_convert_fusion.2
  280.9 26.8 %reduce-scatter.12.cloned.1.call-done = bf16[256,640]{1,0:T(8,128)(2,1)} async-done(((bf16[1024,640]{1,0:T(8,128)(2,1)}), bf16[256,640]{1,0:T(8,128)(2,1)}) %reduce-scatter.12.cloned.1.call-update) | async-done | bytes 327696 | tf_op jit(solution)/shard_map/reduce_scatter | solution.py:143
  312.5 18.1 %all-gather.10.cloned.1.call-done = bf16[1024,640]{1,0:T(8,128)(2,1)} async-done(((bf16[256,640]{1,0:T(8,128)(2,1)}), bf16[1024,640]{1,0:T(8,128)(2,1)}) %all-gather.10.cloned.1.call-update) | async-done | bytes 1310736 | tf_op jit(solution)/shard_map/all_gather | solution.py:150
  330.6 5.2 multiply_convert_fusion.1
  339.6 26.6 %reduce-scatter.14.cloned.1.call-done = bf16[256,640]{1,0:T(8,128)(2,1)} async-done(((bf16[1024,640]{1,0:T(8,128)(2,1)}), bf16[256,640]{1,0:T(8,128)(2,1)}) %reduce-scatter.14.cloned.1.call-update) | async-done | bytes 327696 | tf_op jit(solution)/shard_map/reduce_scatter | solution.py:159
  367.8 2.8 multiply_reduce_fusion.8
  372.5 18.2 %all-gather.12.cloned.1.call-done = bf16[1024,640]{1,0:T(8,128)(2,1)} async-done(((bf16[256,640]{1,0:T(8,128)(2,1)}), bf16[1024,640]{1,0:T(8,128)(2,1)}) %all-gather.12.cloned.1.call-update) | async-done | bytes 1310736 | tf_op jit(solution)/shard_map/all_gather | solution.py:175
  397.8 2.5 multiply_add_fusion.3
  405.6 2.7 reshape.298
  416.0 3.3 fusion.91
  419.4 3.7 fusion.89
  423.2 3.3 fusion.90
  426.9 2.8 fusion.50
  431.5 111.4 %all-reduce.12.cloned.1.call-done = f32[32,10240]{1,0:T(8,128)} async-done(((f32[32,10240]{1,0:T(8,128)}), f32[32,10240]{1,0:T(8,128)}) %all-reduce.12.cloned.1.call-update) | async-done | bytes 1310736
  544.5 26.6 %reduce-scatter.16.cloned.1.call-done = bf16[256,640]{1,0:T(8,128)(2,1)} async-done(((bf16[1024,640]{1,0:T(8,128)(2,1)}), bf16[256,640]{1,0:T(8,128)(2,1)}) %reduce-scatter.16.cloned.1.call-update) | async-done | bytes 327696 | tf_op jit(solution)/shard_map/reduce_scatter | solution.py:203
  572.6 39.9 %all-reduce.9 = (f32[32,80]{1,0:T(8,128)S(1)}, f32[32,16]{1,0:T(8,128)S(1)}) all-reduce(f32[32,80]{1,0:T(8,128)S(1)} %bitcast.62, f32[32,16]{1,0:T(8,128)S(1)} %reshape_transpose_reshape.3), channel_id=12, replica_groups=mesh['dp'=8,'tensor'=4] {'dp','tensor'}, use_global_device_ids=true, to_apply=%region_32.33.clone | all-reduce | flops 3072 | bytes 24576
  615.8 23.6 %reduce-scatter.26.cloned.1.call-done = f32[512,80]{0,1:T(8,128)} async-done(((f32[512,640]{0,1:T(8,128)}), f32[512,80]{0,1:T(8,128)}) %reduce-scatter.26.cloned.1.call-update) | async-done | bytes 163856 | tf_op jit(solution)/shard_map/reduce_scatter | solution.py:168
  639.4 67.4 %reduce-scatter.22.cloned.1.call-done = f32[80,512]{1,0:T(8,128)} async-done(((f32[640,512]{1,0:T(8,128)}), f32[80,512]{1,0:T(8,128)}) %reduce-scatter.22.cloned.1.call-update) | async-done | bytes 163856 | tf_op jit(solution)/shard_map/reduce_scatter | solution.py:166
  706.8 67.2 %reduce-scatter.24.cloned.1.call-done = f32[80,512]{1,0:T(8,128)} async-done(((f32[640,512]{1,0:T(8,128)}), f32[80,512]{1,0:T(8,128)}) %reduce-scatter.24.cloned.1.call-update) | async-done | bytes 163856 | tf_op jit(solution)/shard_map/reduce_scatter | solution.py:167
  774.0 64.9 %reduce-scatter.20.cloned.1.call-done = f32[256,80]{0,1:T(8,128)} async-done(((f32[256,640]{0,1:T(8,128)}), f32[256,80]{0,1:T(8,128)}) %reduce-scatter.20.cloned.1.call-update) | async-done | bytes 81936 | tf_op jit(solution)/shard_map/reduce_scatter | solution.py:216
  838.9 65.3 %reduce-scatter.18.cloned.1.call-done = f32[80,256]{1,0:T(8,128)} async-done(((f32[640,256]{1,0:T(8,128)}), f32[80,256]{1,0:T(8,128)}) %reduce-scatter.18.cloned.1.call-update) | async-done | bytes 81936 | tf_op jit(solution)/shard_map/reduce_scatter | solution.py:215
  (292 shorter events, 62.3 us)
Async XLA Ops:
  7.2 76.6 %copy-start.83 = (f32[2,256]{1,0:T(2,128)S(1)}, f32[2,256]{1,0:T(2,128)}, u32[]{:S(2)}) copy-start(f32[2,256]{1,0:T(2,128)} %param.32) | copy-start | bytes 6148
  7.2 76.6 %copy-start.43 = (bf16[80,512]{1,0:T(8,128)(2,1)S(1)}, bf16[80,512]{1,0:T(8,128)(2,1)}, u32[]{:S(2)}) copy-start(bf16[80,512]{1,0:T(8,128)(2,1)} %param.26) | copy-start | bytes 245764
  7.2 108.2 %all-gather.6.cloned.1.call-start = ((), (), s32[]{:S(2)}) async-start(), calls=%async_computation.9 | async-start | bytes 1638400 | tf_op jit(solution)/shard_map/all_gather | solution.py:82
  12.3 152.1 %reduce-scatter.10.cloned.1.call-start = ((), (), s32[]{:S(2)}) async-start(), calls=%async_computation.10 | async-start | bytes 3276800 | tf_op jit(solution)/shard_map/reduce_scatter | solution.py:129
  18.6 101.5 %copy-start.84 = (f32[128]{0:T(128)}, f32[128]{0:T(128)S(1)}, u32[]{:S(2)}) copy-start(f32[128]{0:T(128)S(1)} %multiply_power_fusion) | copy-start | bytes 1540
  50.6 68.1 %copy-start.19 = (bf16[640,256]{1,0:T(8,128)(2,1)}, bf16[640,256]{1,0:T(8,128)(2,1)S(1)}, u32[]{:S(2)}) copy-start(bf16[640,256]{1,0:T(8,128)(2,1)S(1)} %all_gather.35) | copy-start | bytes 983044
  83.7 35.1 %copy-start.65 = (f32[1,256]{1,0:T(1,128)}, f32[1,256]{1,0:T(1,128)S(1)}, u32[]{:S(2)}) copy-start(f32[1,256]{1,0:T(1,128)S(1)} %get-tuple-element.148) | copy-start | bytes 3076
  83.8 35.1 %copy-start.67 = (f32[1,256]{1,0:T(1,128)}, f32[1,256]{1,0:T(1,128)S(1)}, u32[]{:S(2)}) copy-start(f32[1,256]{1,0:T(1,128)S(1)} %get-tuple-element.149) | copy-start | bytes 3076
  128.5 38.3 %copy-start.8 = (bf16[256,640]{1,0:T(8,128)(2,1)S(1)}, bf16[256,640]{1,0:T(8,128)(2,1)}, u32[]{:S(2)}) copy-start(bf16[256,640]{1,0:T(8,128)(2,1)} %param.23) | copy-start | bytes 983044
  128.5 41.7 %copy-start.44 = (bf16[80,512]{1,0:T(8,128)(2,1)S(1)}, bf16[80,512]{1,0:T(8,128)(2,1)}, u32[]{:S(2)}) copy-start(bf16[80,512]{1,0:T(8,128)(2,1)} %param.28) | copy-start | bytes 245764
  128.5 143.9 %all-gather.8.cloned.1.call-start = ((), (), s32[]{:S(2)}) async-start(), calls=%async_computation.11 | async-start | bytes 1638400 | tf_op jit(solution)/shard_map/all_gather | solution.py:134
  170.2 137.5 %reduce-scatter.12.cloned.1.call-start = ((), (), s32[]{:S(2)}) async-start(), calls=%async_computation.12 | async-start | bytes 1638400 | tf_op jit(solution)/shard_map/reduce_scatter | solution.py:143
  278.8 30.0 %copy-start.50 = (f32[640]{0:T(1024)S(1)}, f32[640]{0:T(1024)}, u32[]{:S(2)}) copy-start(f32[640]{0:T(1024)} %get-tuple-element.126) | copy-start | bytes 7684
  280.9 49.7 %all-gather.10.cloned.1.call-start = ((), (), s32[]{:S(2)}) async-start(), calls=%async_computation.13 | async-start | bytes 1638400 | tf_op jit(solution)/shard_map/all_gather | solution.py:150
  312.2 54.0 %reduce-scatter.14.cloned.1.call-start = ((), (), s32[]{:S(2)}) async-start(), calls=%async_computation.14 | async-start | bytes 1638400 | tf_op jit(solution)/shard_map/reduce_scatter | solution.py:159
  337.4 28.8 %copy-start.47 = (f32[640]{0:T(1024)S(1)}, f32[640]{0:T(1024)}, u32[]{:S(2)}) copy-start(f32[640]{0:T(1024)} %get-tuple-element.129) | copy-start | bytes 7684
  337.4 28.8 %copy-start.64 = (f32[256]{0:T(256)S(1)}, f32[256]{0:T(256)}, u32[]{:S(2)}) copy-start(f32[256]{0:T(256)} %copy-done.63) | copy-start | bytes 3076
  339.5 28.3 %copy-start.45 = (f32[640]{0:T(1024)S(1)}, f32[640]{0:T(1024)}, u32[]{:S(2)}) copy-start(f32[640]{0:T(1024)} %get-tuple-element.127) | copy-start | bytes 7684
  339.5 28.3 %copy-start.62 = (f32[256]{0:T(256)S(1)}, f32[256]{0:T(256)}, u32[]{:S(2)}) copy-start(f32[256]{0:T(256)} %copy-done.61) | copy-start | bytes 3076
  339.5 31.1 %copy-start.72 = (f32[256]{0:T(256)S(1)}, f32[256]{0:T(256)}, u32[]{:S(2)}) copy-start(f32[256]{0:T(256)} %copy-done.71) | copy-start | bytes 3076
  339.5 51.3 %all-gather.12.cloned.1.call-start = ((), (), s32[]{:S(2)}) async-start(), calls=%async_computation.15 | async-start | bytes 1638400 | tf_op jit(solution)/shard_map/all_gather | solution.py:175
  372.4 170.5 %all-reduce.12.cloned.1.call-start = ((), (), s32[]{:S(2)}) async-start(), calls=%async_computation.22 | async-start | bytes 2621440
  411.3 159.9 %reduce-scatter.16.cloned.1.call-start = ((), (), s32[]{:S(2)}) async-start(), calls=%async_computation.16 | async-start | bytes 1638400 | tf_op jit(solution)/shard_map/reduce_scatter | solution.py:203
  415.9 223.5 %reduce-scatter.26.cloned.1.call-start = ((), (), s32[]{:S(2)}) async-start(), calls=%async_computation.21 | async-start | bytes 1474560 | tf_op jit(solution)/shard_map/reduce_scatter | solution.py:168
  419.4 287.5 %reduce-scatter.22.cloned.1.call-start = ((), (), s32[]{:S(2)}) async-start(), calls=%async_computation.19 | async-start | bytes 1474560 | tf_op jit(solution)/shard_map/reduce_scatter | solution.py:166
  423.2 350.9 %reduce-scatter.24.cloned.1.call-start = ((), (), s32[]{:S(2)}) async-start(), calls=%async_computation.20 | async-start | bytes 1474560 | tf_op jit(solution)/shard_map/reduce_scatter | solution.py:167
  426.6 412.3 %reduce-scatter.20.cloned.1.call-start = ((), (), s32[]{:S(2)}) async-start(), calls=%async_computation.18 | async-start | bytes 737280 | tf_op jit(solution)/shard_map/reduce_scatter | solution.py:216
  429.7 141.5 %copy-start.49 = (f32[640]{0:T(1024)S(1)}, f32[640]{0:T(1024)}, u32[]{:S(2)}) copy-start(f32[640]{0:T(1024)} %copy-done.48) | copy-start | bytes 7684
  429.7 141.5 %copy-start.60 = (f32[256]{0:T(256)S(1)}, f32[256]{0:T(256)}, u32[]{:S(2)}) copy-start(f32[256]{0:T(256)} %copy-done.59) | copy-start | bytes 3076
  429.7 474.4 %reduce-scatter.18.cloned.1.call-start = ((), (), s32[]{:S(2)}) async-start(), calls=%async_computation.17 | async-start | bytes 737280 | tf_op jit(solution)/shard_map/reduce_scatter | solution.py:215
  429.9 183.8 %copy-start.70 = (f32[256]{0:T(256)S(1)}, f32[256]{0:T(256)}, u32[]{:S(2)}) copy-start(f32[256]{0:T(256)} %copy-done.69) | copy-start | bytes 3076
  430.0 183.8 %copy-start.10 = (f32[256,640]{1,0:T(8,128)S(1)}, f32[256,640]{1,0:T(8,128)}, u32[]{:S(2)}) copy-start(f32[256,640]{1,0:T(8,128)} %copy-done.9) | copy-start | bytes 1966084
  (72 other events, 191.3 us)
Sparse Core Ops, SparseCore 0:
  12.4 20.8 all-gather.5
  128.6 35.7 reduce-scatter.9
  170.3 18.1 all-gather.7
  281.0 26.6 reduce-scatter.11
  312.3 18.1 all-gather.9
  339.6 26.5 reduce-scatter.13
  372.5 18.1 all-gather.11
  411.4 131.4 all-reduce.11
  545.6 25.4 reduce-scatter.15
  575.0 64.3 reduce-scatter.25
  643.4 63.4 reduce-scatter.21
  710.7 63.3 reduce-scatter.23
  777.9 60.9 reduce-scatter.19
  842.9 61.1 reduce-scatter.17
where the time goes:
time: 912 us; the launch traced here: 911 us
  waiting for transfers between devices  552 us (61%)
  blocking collectives  245 us (27%)
  matrix products  47.7 us (5%)
  other arithmetic  28.9 us (3%)
  local copies, waits for them, and re-layouts  20.8 us (2%)
  between operations  15.1 us (2%)
    unnamed x15, waiting for transfers between devices  112 us
    reduce_scatter x1, waiting for transfers between devices, body(): lax.psum_scatter(gate_grad, 'dp', scatter_dimension=0, tiled=True)  67.4 us
    reduce_scatter x1, waiting for transfers between devices, body(): lax.psum_scatter(up_grad, 'dp', scatter_dimension=0, tiled=True)  67.2 us
    reduce_scatter x1, waiting for transfers between devices, body(): lax.psum_scatter(query_grad, 'dp', scatter_dimension=0, tiled=True)  65.3 us
    reduce_scatter x1, waiting for transfers between devices, body(): lax.psum_scatter(output_grad, 'dp', scatter_dimension=1, tiled=True)  64.9 us
    unnamed x1, blocking collectives  39.9 us
    reduce_scatter x1, waiting for transfers between devices, body(): lax.psum_scatter(dot_rows(attended, output_full), 'tensor', scatter_dimen...  35.9 us
    all_gather x1, blocking collectives, body(): lax.all_gather(up_weight, 'dp', axis=0, tiled=True)  34.1 us
  transfers between devices with their start and end apart: 14, of which 12 were waited for; matrix products, arithmetic and copies ran while one was open for 3% of the time, Pallas kernels for 0%

commit v1 on v0

v1 whole, which is shorter than its diff:
```python
import functools

import jax
import jax.numpy as jnp
from jax import lax
from jax.experimental import pallas as pl
from jax.experimental.pallas import tpu as pltpu
from jax.sharding import PartitionSpec as P

epsilon = 1e-06
rope_base = 1000000.0
score_scale = 0.0625
MESH = pl.DeviceIdType.MESH
chunk_count = 4
vmem_bytes = 56 * 2**20
in_vmem = pl.BlockSpec(memory_space=pltpu.VMEM)


def norm_rows(values, scaling):
    return values * lax.rsqrt(jnp.mean(values * values, axis=-1, keepdims=True) + epsilon) * scaling


def norm_pull(values, scaling, grad):
    inverse = lax.rsqrt(jnp.mean(values * values, axis=-1, keepdims=True) + epsilon)
    scaled = grad * scaling
    inner = jnp.mean(values * scaled, axis=-1, keepdims=True)
    pulled = inverse * scaled - values * (inverse * inverse * inverse * inner)
    return pulled, jnp.sum(grad * values * inverse, axis=0, keepdims=True)


def angles(length, head_width):
    halfway = head_width // 2
    places = jnp.arange(length, dtype=jnp.float32)[:, None]
    frequency = rope_base ** (-2.0 * jnp.arange(halfway, dtype=jnp.float32) / head_width)
    phases = places * frequency[None, :]
    return (jnp.cos(phases), jnp.sin(phases))


def rotate(values, cosine_table, sine_table):
    halfway = values.shape[-1] // 2
    leading = values[..., :halfway]
    trailing = values[..., halfway:]
    return jnp.concatenate(
        [
            leading * cosine_table - trailing * sine_table,
            trailing * cosine_table + leading * sine_table,
        ],
        axis=-1,
    )


def activate(gating, upward):
    return jax.nn.gelu(gating, approximate=True) * upward


def dot_rows(left_side, right_side):
    return jnp.dot(left_side, right_side, preferred_element_type=jnp.float32)


def dot_inner(left_side, right_side):
    return lax.dot_general(
        left_side, right_side, (((1,), (1,)), ((), ())), preferred_element_type=jnp.float32
    )


def dot_outer(left_side, right_side):
    return lax.dot_general(
        left_side, right_side, (((0,), (0,)), ((), ())), preferred_element_type=jnp.float32
    )


def send(source, target, send_sem, recv_sem, device):
    return pltpu.make_async_remote_copy(
        src_ref=source,
        dst_ref=target,
        send_sem=send_sem,
        recv_sem=recv_sem,
        device_id=device,
        device_id_type=MESH,
    )


def tensor_peers():
    me = lax.axis_index("tensor")
    chip = me // 2
    core = me % 2
    mate = chip * 2 + 1 - core
    across = (1 - chip) * 2 + core
    diagonal = (1 - chip) * 2 + 1 - core
    return me, mate, across, diagonal


def ring_place(index, count):
    odd = index % 2
    return (index // 2) * (1 - odd) + (count - 1 - index // 2) * odd


def ring_index(place, count):
    back = place // (count // 2)
    return (2 * place) * (1 - back) + (2 * (count - 1 - place) + 1) * back


def greet(targets):
    barrier = pltpu.get_barrier_semaphore()
    for target in targets:
        pl.semaphore_signal(barrier, inc=1, device_id=target, device_id_type=MESH)
    pl.semaphore_wait(barrier, len(targets))


def call(kernel, arguments, outputs, scratch, collective_id):
    return pl.pallas_call(
        kernel,
        out_shape=outputs,
        in_specs=[in_vmem] * len(arguments),
        out_specs=[in_vmem] * len(outputs),
        scratch_shapes=scratch,
        compiler_params=pltpu.CompilerParams(
            collective_id=collective_id, has_side_effects=True, vmem_limit_bytes=vmem_bytes
        ),
    )(*arguments)


class Spread:
    def __init__(self, gathered, send_sems, recv_sems, rows):
        self.gathered, self.send_sems, self.recv_sems, self.rows = gathered, send_sems, recv_sems, rows
        self.me, self.mate, self.across, self.diagonal = tensor_peers()
        self.sent = []

    def copy(self, flow, owner, chunk, device):
        part = self.gathered.at[owner, pl.ds(chunk * self.rows, self.rows)]
        return send(
            part, part, self.send_sems.at[flow, chunk], self.recv_sems.at[flow, chunk], {"tensor": device}
        )

    def give(self, chunk):
        for flow, device in ((0, self.across), (1, self.mate)):
            copy = self.copy(flow, self.me, chunk, device)
            copy.start()
            self.sent.append(copy)

    def forward(self, chunk):
        self.copy(0, self.across, chunk, self.across).wait_recv()
        copy = self.copy(2, self.across, chunk, self.mate)
        copy.start()
        self.sent.append(copy)

    def finish(self, chunks):
        for chunk in range(chunks):
            self.copy(1, self.mate, chunk, self.mate).wait_recv()
            self.copy(2, self.diagonal, chunk, self.mate).wait_recv()
        for copy in self.sent:
            copy.wait_send()


def opening_kernel(
    count, tokens, segments, gains, shard, rows_all, segment_all, full, send_sems, recv_sems, seg_send, seg_recv, ring_send, ring_recv
):
    me, mate, across, diagonal = tensor_peers()
    mine = lax.axis_index("dp")
    place = ring_place(mine, count)
    right = ring_index((place + 1) % count, count)
    left = ring_index((place + count - 1) % count, count)
    greet([{"tensor": mate}, {"tensor": across}, {"tensor": diagonal}, {"dp": right}, {"dp": left}])
    full[mine] = shard[...]
    segment_all[me] = segments[...]
    half = shard.shape[1] // 2
    last = count // 2 - 1

    def ring_copy(way, step, owner):
        device = {"dp": left if way else right}
        part = full.at[owner]
        if step == last:
            part = full.at[owner, :, pl.ds(half * way, half)]
        return send(part, part, ring_send.at[way, step], ring_recv.at[way, step], device)

    def ring_owner(way, step):
        shift = step if way else count - step
        return ring_index((place + shift) % count, count)

    ring_sent = []

    def ring_start(step):
        for way in (0, 1):
            if step > 0:
                ring_copy(way, step - 1, ring_owner(way, step)).wait_recv()
            if step <= last:
                copy = ring_copy(way, step, ring_owner(way, step))
                copy.start()
                ring_sent.append(copy)

    ring_start(0)
    spread = Spread(rows_all, send_sems, recv_sems, tokens.shape[0] // chunk_count)
    for chunk in range(chunk_count):
        rows = pl.ds(chunk * spread.rows, spread.rows)
        normed = norm_rows(tokens[rows, :].astype(jnp.float32), gains[0:1, :])
        rows_all[me, rows, :] = normed.astype(jnp.bfloat16)
        spread.give(chunk)
    seg_sent = []
    for flow, device in enumerate((mate, across, diagonal)):
        part = segment_all.at[me]
        copy = send(part, part, seg_send.at[flow], seg_recv.at[flow], {"tensor": device})
        copy.start()
        seg_sent.append(copy)
    for chunk in range(chunk_count):
        spread.forward(chunk)
    for step in range(1, last + 2):
        ring_start(step)
    spread.finish(chunk_count)
    for flow, device in enumerate((mate, across, diagonal)):
        part = segment_all.at[device]
        send(part, part, seg_send.at[flow], seg_recv.at[flow], {"tensor": device}).wait_recv()
    for copy in seg_sent + ring_sent:
        copy.wait_send()


def opening(tokens, segments, gains, shard, count):
    rows, width = tokens.shape
    return call(
        functools.partial(opening_kernel, count),
        (tokens, segments, gains, shard),
        [
            jax.ShapeDtypeStruct((4, rows, width), jnp.bfloat16),
            jax.ShapeDtypeStruct((4,) + segments.shape, jnp.int32),
            jax.ShapeDtypeStruct((count,) + shard.shape, jnp.bfloat16),
        ],
        [
            pltpu.SemaphoreType.DMA((3, chunk_count)),
            pltpu.SemaphoreType.DMA((3, chunk_count)),
            pltpu.SemaphoreType.DMA((3,)),
            pltpu.SemaphoreType.DMA((3,)),
            pltpu.SemaphoreType.DMA((2, count // 2)),
            pltpu.SemaphoreType.DMA((2, count // 2)),
        ],
        0,
    )


def joint_kernel(row_map, extra_count, row_count, sum_count, spreads, *refs):
    refs = list(refs)

    def take(number):
        taken = refs[:number]
        del refs[:number]
        return taken

    (partial,) = take(1)
    extras = take(extra_count)
    (gains,) = take(1)
    gathered = take(1)[0] if spreads else None
    row_outs = take(row_count)
    sum_outs = take(sum_count)
    near, outgoing, far, send_sems, recv_sems = take(5)
    if spreads:
        spread_send, spread_recv = take(2)
    me, mate, across, diagonal = tensor_peers()
    rows_each = partial.shape[1] // chunk_count
    greet([{"tensor": mate}, {"tensor": across}])

    def near_copy(flow, chunk):
        owner = mate if flow else diagonal
        part = pl.ds(chunk * rows_each, rows_each)
        return send(
            partial.at[owner, part], near.at[flow, part], send_sems.at[flow, chunk], recv_sems.at[flow, chunk], {"tensor": mate}
        )

    def far_copy(chunk):
        part = pl.ds(chunk * rows_each, rows_each)
        return send(outgoing.at[part], far.at[part], send_sems.at[2, chunk], recv_sems.at[2, chunk], {"tensor": across})

    for flow in (0, 1):
        for chunk in range(chunk_count):
            near_copy(flow, chunk).start()
    for chunk in range(chunk_count):
        part = pl.ds(chunk * rows_each, rows_each)
        near_copy(0, chunk).wait_recv()
        total = partial[across, part, :].astype(jnp.float32) + near[0, part, :].astype(jnp.float32)
        outgoing[part, :] = total.astype(jnp.bfloat16)
        far_copy(chunk).start()
    if spreads:
        spread = Spread(gathered, spread_send, spread_recv, rows_each)
    sums = None
    for chunk in range(chunk_count):
        part = pl.ds(chunk * rows_each, rows_each)
        near_copy(1, chunk).wait_recv()
        total = partial[me, part, :].astype(jnp.float32) + near[1, part, :].astype(jnp.float32)
        far_copy(chunk).wait_recv()
        total = total + far[part, :].astype(jnp.float32)
        given, rows_out, sums_out = row_map(total, [extra[part, :] for extra in extras], gains)
        if spreads:
            gathered[me, part, :] = given.astype(jnp.bfloat16)
            spread.give(chunk)
        for ref, value in zip(row_outs, rows_out):
            ref[part, :] = value.astype(ref.dtype)
        sums = sums_out if sums is None else [held + new for held, new in zip(sums, sums_out)]
        if spreads and chunk > 0:
            spread.forward(chunk - 1)
    for ref, value in zip(sum_outs, sums):
        ref[...] = value
    if spreads:
        spread.forward(chunk_count - 1)
        spread.finish(chunk_count)
    for chunk in range(chunk_count):
        near_copy(0, chunk).wait_send()
        near_copy(1, chunk).wait_send()
        far_copy(chunk).wait_send()


def joint(row_map, partial, extras, gains, row_types, sum_count, spreads, collective_id):
    rows, width = partial.shape[0] // 4, partial.shape[1]
    outputs = []
    if spreads:
        outputs.append(jax.ShapeDtypeStruct((4, rows, width), jnp.bfloat16))
    outputs += [jax.ShapeDtypeStruct((rows, width), kind) for kind in row_types]
    outputs += [jax.ShapeDtypeStruct((1, width), jnp.float32)] * sum_count
    scratch = [
        pltpu.VMEM((2, rows, width), jnp.bfloat16),
        pltpu.VMEM((rows, width), jnp.bfloat16),
        pltpu.VMEM((rows, width), jnp.bfloat16),
        pltpu.SemaphoreType.DMA((3, chunk_count)),
        pltpu.SemaphoreType.DMA((3, chunk_count)),
    ]
    if spreads:
        scratch += [pltpu.SemaphoreType.DMA((3, chunk_count))] * 2
    found = list(call(
        functools.partial(joint_kernel, row_map, len(extras), len(row_types), sum_count, spreads),
        (partial.reshape(4, rows, width),) + tuple(extras) + (gains,),
        outputs,
        scratch,
        collective_id,
    ))
    if spreads:
        found[0] = found[0].reshape(4 * rows, width)
    return found


def branch_map(branch, extras, gains):
    middle = extras[0].astype(jnp.float32) + norm_rows(branch, gains[1:2, :])
    return norm_rows(middle, gains[2:3, :]), [branch, middle], []


def ffn_map(ffn_out, extras, gains):
    middle, cotangent = extras
    outcome = middle + norm_rows(ffn_out, gains[3:4, :])
    grad_ffn, gain_last = norm_pull(ffn_out, gains[3:4, :], cotangent.astype(jnp.float32))
    return grad_ffn, [outcome], [gain_last]


def middle_map(grad_mid_normed, extras, gains):
    middle, branch, cotangent = extras
    pulled, gain_mid = norm_pull(middle, gains[2:3, :], grad_mid_normed)
    grad_middle = cotangent.astype(jnp.float32) + pulled
    grad_branch, gain_branch = norm_pull(branch, gains[1:2, :], grad_middle)
    return grad_branch, [grad_middle], [gain_branch, gain_mid]


def first_map(grad_first_normed, extras, gains):
    tokens, grad_middle = extras
    pulled, gain_first = norm_pull(tokens.astype(jnp.float32), gains[0:1, :], grad_first_normed)
    return None, [grad_middle + pulled], [gain_first]


def closing_kernel(count, split, shared, grads, summed, joined, slots_a, slots_b, staged, arrived, send_sems, recv_sems, tail_send, tail_recv):
    me = lax.axis_index("tensor")
    mine = lax.axis_index("dp")
    place = ring_place(mine, count)
    right = ring_index((place + 1) % count, count)
    left = ring_index((place + count - 1) % count, count)
    others = [(me + shift) % 4 for shift in (1, 2, 3)]
    greet([{"dp": right}, {"dp": left}] + [{"tensor": other} for other in others])
    width = grads.shape[2]
    ways = ((0, split), (split, width - split))

    def chunk_index(way, step):
        shift = 1 + step if way else 2 * count - 1 - step
        return ring_index((place + shift) % count, count)

    def ring_copy(way, step):
        slots = slots_b if way else slots_a
        start, size = ways[way]
        if step == 0:
            source = grads.at[chunk_index(way, 0), :, pl.ds(start, size)]
        else:
            source = slots.at[step - 1]
        return send(source, slots.at[step], send_sems.at[way, step], recv_sems.at[way, step], {"dp": left if way else right})

    for way in (0, 1):
        ring_copy(way, 0).start()
    for step in range(1, count):
        for way in (0, 1):
            slots = slots_b if way else slots_a
            start, size = ways[way]
            ring_copy(way, step - 1).wait_recv()
            total = slots[step - 1].astype(jnp.float32) + grads[chunk_index(way, step), :, pl.ds(start, size)].astype(jnp.float32)
            if step < count - 1:
                slots[step - 1] = total.astype(jnp.bfloat16)
                ring_copy(way, step).start()
            else:
                summed[:, pl.ds(start, size)] = total
    first, each, tail = shared
    for device in range(4):
        staged[device, :, pl.ds(0, each)] = summed[:, pl.ds(first + each * device, each)]
        staged[device, :, pl.ds(each, tail)] = summed[:, pl.ds(width - tail, tail)]
    tails = []
    for slot, other in enumerate(others):
        copy = send(staged.at[other], arrived.at[slot], tail_send.at[slot], tail_recv.at[slot], {"tensor": other})
        copy.start()
        tails.append(copy)
    total = staged[me]
    for slot in range(3):
        tails[slot].wait_recv()
        total = total + arrived[slot]
    joined[...] = total
    for copy in tails:
        copy.wait_send()
    for step in range(count - 1):
        for way in (0, 1):
            ring_copy(way, step).wait_send()


def closing(grads, shared, split, count):
    rows, width = grads.shape[1:]
    block = shared[1] + shared[2]
    return call(
        functools.partial(closing_kernel, count, split, shared),
        (grads,),
        [
            jax.ShapeDtypeStruct((rows, width), jnp.float32),
            jax.ShapeDtypeStruct((rows, block), jnp.float32),
        ],
        [
            pltpu.VMEM((count - 1, rows, split), jnp.bfloat16),
            pltpu.VMEM((count - 1, rows, width - split), jnp.bfloat16),
            pltpu.VMEM((4, rows, block), jnp.float32),
            pltpu.VMEM((3, rows, block), jnp.float32),
            pltpu.SemaphoreType.DMA((2, count - 1)),
            pltpu.SemaphoreType.DMA((2, count - 1)),
            pltpu.SemaphoreType.DMA((3,)),
            pltpu.SemaphoreType.DMA((3,)),
        ],
        5,
    )


def body(
    tokens,
    segments,
    query_weight,
    keyvalue_weight,
    output_weight,
    gate_weight,
    up_weight,
    down_weight,
    norm_gains,
    headnorm_gains,
    cotangent,
):
    head_width = headnorm_gains.shape[1]
    width = tokens.shape[1]
    hidden_width = gate_weight.shape[1]
    count = lax.axis_size("dp")
    own_rows = query_weight.shape[0]
    padded_rows = -(-own_rows // 16) * 16
    shard = jnp.concatenate(
        [query_weight, keyvalue_weight, output_weight.T, gate_weight, up_weight, down_weight.T], axis=1
    )
    shard = jnp.pad(shard, ((0, padded_rows - own_rows), (0, 0)))
    seg_tile = segments.reshape(-1, 128)
    seg_rows = seg_tile.shape[0]
    seg_tile = jnp.pad(seg_tile, ((0, 8 - seg_rows), (0, 0)))
    rows_all, segment_all, full = opening(tokens, seg_tile, norm_gains, shard, count)
    rows_all = rows_all.reshape(-1, width)
    segment_all = segment_all[:, :seg_rows].reshape(-1)
    full = full[:, :own_rows].reshape(width, -1)
    ends = [0, head_width, 3 * head_width, 4 * head_width, 4 * head_width + 2 * hidden_width, 4 * head_width + 3 * hidden_width]
    mixed_full = full[:, : ends[2]]
    output_full = full[:, ends[2] : ends[3]]
    pair_full = full[:, ends[3] : ends[4]]
    down_full = full[:, ends[4] : ends[5]]
    length = rows_all.shape[0]
    block_rows = min(512, length)
    cosine_table, sine_table = angles(length, head_width)

    def query_map(raw_values, scaling):
        return rotate(norm_rows(raw_values, scaling), cosine_table, sine_table) * score_scale

    def key_map(raw_values, scaling):
        return rotate(norm_rows(raw_values, scaling), cosine_table, sine_table)

    mixed_raw = dot_rows(rows_all, mixed_full)
    query_raw = mixed_raw[:, :head_width]
    keyvalue_raw = mixed_raw[:, head_width:]
    query_rows = query_map(query_raw, headnorm_gains[0]).astype(jnp.bfloat16)
    key_rows = key_map(keyvalue_raw[:, :head_width], headnorm_gains[1]).astype(jnp.bfloat16)
    value_rows = keyvalue_raw[:, head_width:].astype(jnp.bfloat16)

    def masked_scores(row_from, row_to):
        scores = dot_inner(query_rows[row_from:row_to], key_rows[:row_to])
        row_places = row_from + jnp.arange(row_to - row_from)
        key_places = jnp.arange(row_to)
        allowed = (key_places[None, :] <= row_places[:, None]) & (
            segment_all[row_from:row_to][:, None] == segment_all[:row_to][None, :]
        )
        return jnp.where(allowed, scores, -jnp.inf)

    pieces_out = []
    pieces_total = []
    for block_id in range(length // block_rows):
        row_from = block_id * block_rows
        row_to = row_from + block_rows
        scores = masked_scores(row_from, row_to)
        row_peak = jnp.max(scores, axis=-1, keepdims=True)
        raised = jnp.exp(scores - row_peak)
        row_total = jnp.sum(raised, axis=-1, keepdims=True)
        weights_low = (raised / row_total).astype(jnp.bfloat16)
        pieces_out.append(dot_rows(weights_low, value_rows[:row_to]).astype(jnp.bfloat16))
        pieces_total.append(row_peak + jnp.log(row_total))
    attended = jnp.concatenate(pieces_out, axis=0)
    log_totals = jnp.concatenate(pieces_total, axis=0)
    branch_partial = dot_inner(attended, output_full).astype(jnp.bfloat16)
    mid_all, branch, middle = joint(
        branch_map, branch_partial, (tokens,), norm_gains, (jnp.float32, jnp.float32), 0, True, 1
    )
    paired = dot_rows(mid_all, pair_full)
    gating = paired[:, :hidden_width]
    upward = paired[:, hidden_width:]
    hidden = activate(gating, upward).astype(jnp.bfloat16)
    ffn_partial = dot_inner(hidden, down_full).astype(jnp.bfloat16)
    grad_ffn_all, outcome, gain_last = joint(
        ffn_map, ffn_partial, (middle, cotangent), norm_gains, (jnp.bfloat16,), 1, True, 2
    )
    grad_hidden = dot_rows(grad_ffn_all, down_full)
    down_grad = dot_outer(grad_ffn_all, hidden).astype(jnp.bfloat16)
    ignored, pull_active = jax.vjp(activate, gating, upward)
    grad_gating, grad_upward = pull_active(grad_hidden)
    paired_low = jnp.concatenate(
        [grad_gating.astype(jnp.bfloat16), grad_upward.astype(jnp.bfloat16)], axis=1
    )
    mid_partial = dot_inner(paired_low, pair_full).astype(jnp.bfloat16)
    branch_all, grad_middle, gain_branch, gain_mid = joint(
        middle_map, mid_partial, (middle, branch, cotangent), norm_gains, (jnp.float32,), 2, True, 3
    )
    pair_grad = dot_outer(mid_all, paired_low).astype(jnp.bfloat16)
    output_grad = dot_outer(branch_all, attended).astype(jnp.bfloat16)
    grad_attended = dot_rows(branch_all, output_full).astype(jnp.bfloat16)
    grad_query_parts = []
    grad_keys = jnp.zeros((length, head_width), jnp.float32)
    grad_values = jnp.zeros((length, head_width), jnp.float32)
    for block_id in range(length // block_rows):
        row_from = block_id * block_rows
        row_to = row_from + block_rows
        scores = masked_scores(row_from, row_to)
        weights_full = jnp.exp(scores - log_totals[row_from:row_to])
        weights_low = weights_full.astype(jnp.bfloat16)
        grad_block = grad_attended[row_from:row_to]
        grad_weights = dot_inner(grad_block, value_rows[:row_to])
        row_inner = jnp.sum(weights_full * grad_weights, axis=-1, keepdims=True)
        grad_scores = (weights_full * (grad_weights - row_inner)).astype(jnp.bfloat16)
        grad_query_parts.append(dot_rows(grad_scores, key_rows[:row_to]))
        grad_keys = grad_keys.at[:row_to].add(dot_outer(grad_scores, query_rows[row_from:row_to]))
        grad_values = grad_values.at[:row_to].add(dot_outer(weights_low, grad_block))
    grad_query = jnp.concatenate(grad_query_parts, axis=0)
    ignored, pull_query = jax.vjp(query_map, query_raw, headnorm_gains[0])
    grad_query_raw, gain_query = pull_query(grad_query)
    ignored, pull_key = jax.vjp(key_map, keyvalue_raw[:, :head_width], headnorm_gains[1])
    grad_key_raw, gain_key = pull_key(grad_keys)
    mixed_low = jnp.concatenate([grad_query_raw, grad_key_raw, grad_values], axis=1).astype(jnp.bfloat16)
    first_partial = dot_inner(mixed_low, mixed_full).astype(jnp.bfloat16)
    grad_tokens, gain_first = joint(
        first_map, first_partial, (tokens, grad_middle), norm_gains, (jnp.float32,), 1, False, 4
    )
    mixed_grad = dot_outer(rows_all, mixed_low).astype(jnp.bfloat16)
    gain_columns = jnp.concatenate([gain_first, gain_branch, gain_mid, gain_last], axis=0).T
    head_each = head_width // count
    head_columns = jnp.stack([gain_query, gain_key], axis=1).reshape(count, head_each, 2)
    head_columns = jnp.pad(head_columns, ((0, 0), (0, own_rows - head_each), (0, 0)))
    gain_tile = jnp.concatenate([gain_columns, head_columns.reshape(width, 2)], axis=1)
    gain_tile = jnp.pad(gain_tile, ((0, 0), (0, 128 - gain_tile.shape[1]))).astype(jnp.bfloat16)
    grads = jnp.concatenate([mixed_grad, output_grad, pair_grad, down_grad, gain_tile], axis=1)
    grads = grads.reshape(count, own_rows, -1)
    grads = jnp.pad(grads, ((0, 0), (0, padded_rows - own_rows), (0, 0)))
    kv_each = keyvalue_weight.shape[1] // 4
    split = grads.shape[2] // 256 * 128
    summed, joined = closing(grads, (head_width, kv_each, 128), split, count)
    summed = summed[:own_rows]
    joined = joined[:own_rows]
    me = lax.axis_index("tensor")
    gains_part = lax.dynamic_slice(joined[:, kv_each : kv_each + 4].T, (me, 0), (1, own_rows))
    head_own = head_each // 4
    heads_part = lax.dynamic_slice(joined[:, kv_each + 4 : kv_each + 6].T, (0, me * head_own), (2, head_own))
    middle_at = ends[3] + hidden_width
    return (
        outcome,
        grad_tokens,
        summed[:, : ends[1]],
        joined[:, :kv_each],
        summed[:, ends[2] : ends[3]].T,
        summed[:, ends[3] : middle_at],
        summed[:, middle_at : ends[4]],
        summed[:, ends[4] : ends[5]].T,
        gains_part,
        heads_part,
    )


def solution(mesh):
    placed = (
        P(("dp", "tensor"), None),
        P(("dp", "tensor")),
        P("dp", "tensor"),
        P("dp", None),
        P("tensor", "dp"),
        P("dp", "tensor"),
        P("dp", "tensor"),
        P("tensor", "dp"),
        P(),
        P(),
        P(("dp", "tensor"), None),
    )
    return jax.shard_map(
        body,
        mesh=mesh,
        in_specs=placed,
        out_specs=(
            P(("dp", "tensor"), None),
            P(("dp", "tensor"), None),
            P("dp", "tensor"),
            P("dp", "tensor"),
            P("tensor", "dp"),
            P("dp", "tensor"),
            P("dp", "tensor"),
            P("tensor", "dp"),
            P("tensor", "dp"),
            P(None, ("dp", "tensor")),
        ),
        check_vma=False,
    )
```

time: 912 us -> 262 us (0.29)
  waiting for transfers between devices: 552 us -> 0 us
  blocking collectives: 245 us -> 0 us
  Pallas kernels: 0 us -> 179 us
  other arithmetic: 28.9 us -> 10.1 us
  between operations: 15.1 us -> 1.32 us
    reduce_scatter x9 -> x0, waiting for transfers between devices: 404 us -> none  [the longest x1 67.4 us: body(): lax.psum_scatter(gate_grad, 'dp', scatter_dimension=0, tiled=True)]
    all_gather x7 -> x0, blocking collectives: 205 us -> none  [the longest x1 34.1 us: body(): lax.all_gather(up_weight, 'dp', axis=0, tiled=True)]
    pallas_call x0 -> x6, Pallas kernels: none -> 179 us  [call(): pl.pallas_call(kernel, out_shape=outputs, in_specs=[in_vmem] * len(argume...]
    unnamed x15 -> x0, waiting for transfers between devices: 112 us -> none
    unnamed x1 -> x0, blocking collectives: 39.9 us -> none
    all_gather x4 -> x0, waiting for transfers between devices: 36.3 us -> none  [the longest x1 18.2 us: body(): lax.all_gather(grad_branch.astype(jnp.bfloat16), 'tensor', axis=0, tiled=...]
    dot_general x10 -> x8, matrix products: 18.2 us -> 12.4 us  [dot_outer(): lax.dot_general(left_side, right_side, (((0,), (0,)), ((), ())), preferre...]
  transfers between devices with their start and end apart: 14 -> 0, of which waited for: 12 -> 0; matrix products, arithmetic and copies ran while one was open for 3% -> 0% of each run, Pallas kernels for 0% -> 0%
where the time goes in v1:
time: 262 us; the launch traced here: 261 us
  Pallas kernels  179 us (68%)
  matrix products  44 us (17%)
  local copies, waits for them, and re-layouts  26.4 us (10%)
  other arithmetic  10.1 us (4%)
    pallas_call x6, Pallas kernels, call(): pl.pallas_call(kernel, out_shape=outputs, in_specs=[in_vmem] * len(argume...  179 us
    dot_general x8, matrix products, dot_inner(): lax.dot_general(left_side, right_side, (((1,), (1,)), ((), ())), preferre...  17.1 us
    dot_general x8, matrix products, dot_rows(): return jnp.dot(left_side, right_side, preferred_element_type=jnp.float32)  14.4 us
    unnamed x80, local copies, waits for them, and re-layouts  13.4 us
    dot_general x8, matrix products, dot_outer(): lax.dot_general(left_side, right_side, (((0,), (0,)), ((), ())), preferre...  12.4 us

profile of v1, /device:TPU:0, one launch (start us, length us, event | category | flops | bytes accessed | tf_op | source)
XLA Modules:
  0.0 260.6 jit_solution(14521980292630313367)
XLA Ops:
  1.4 1.3 pad.38.segments
  3.5 0.9 constant_dynamic-update-slice_fusion.2
  5.2 0.9 constant_dynamic-update-slice_fusion.1
  6.1 0.9 constant_dynamic-update-slice_fusion
  8.6 44.5 %shard_map.196 = (bf16[4,256,640]{2,1,0:T(8,128)(2,1)}, s32[4,8,128]{2,1,0:T(8,128)}, bf16[8,80,2560]{2,1,0:T(8,128)(2,1)}) custom-call(bf16[256,640]{1,0:T(8,128)(2,1)} %refs_1_.3, s32[8,128]{1,0:T(8,128)} %pad.38.segments, f32[4,640]{1,0:T(4,128)} %refs_3_.5, bf16[80,2560]{1,0:T(8,128)(2,1)} %copy-done.23), custom_call_target="tpu_custom_call" | custom-call | tf_op jit(solution)/shard_map/pallas_call | solution.py:111
  54.5 3.0 %fusion.75 = (bf16[1024,768]{0,1:T(8,128)(2,1)S(1)}, f32[1024,768]{0,1:T(8,128)S(1)}) fusion(bf16[1024,640]{1,0:T(8,128)(2,1)} %bitcast.50, bf16[640,2560]{1,0:T(8,128)(2,1)} %bitcast.52), kind=kOutput, calls=%fused_computation.155 | convolution fusion | flops 1007419392 | bytes 7012352 | tf_op jit(solution)/shard_map/dot_general | solution.py:57
  58.0 2.6 %multiply_subtract_fusion = (f32[1024,128]{0,1:T(8,128)S(1)}, f32[1024,128]{0,1:T(8,128)S(1)}, bf16[1024,128]{0,1:T(8,128)(2,1)S(1)}, bf16[1024,128]{0,1:T(8,128)(2,1)S(1)}) fusion(f32[1024,256]{0,1:T(8,128)S(1)} %get-tuple-element.140, f32[128]{0:T(128)S(1)} %multiply_power_fusion, f32[1024,256]{0,1:T(8,128)S(1)} %get-tuple-element.141), kind=kLoop, calls=%fused_computation.89 | loop fusion | flops 1966080 | bytes 3670528 | tf_op jit(solution)/shard_map/sub | solution.py:45
  64.7 2.6 %convolution_convert_fusion = bf16[1024,640]{1,0:T(8,128)(2,1)} fusion(bf16[512,256]{1,0:T(8,128)(2,1)S(1)} %convolution_convert_fusion.9, bf16[512,256]{1,0:T(8,128)(2,1)S(1)} %convolution_convert_fusion.10, bf16[640,2560]{1,0:T(8,128)(2,1)} %bitcast.53), kind=kOutput, calls=%fused_computation.23 | convolution fusion | flops 337248256 | bytes 2162688 | tf_op jit(solution)/shard_map/dot_general | solution.py:61
  67.3 22.8 %shard_map.197 = (bf16[4,256,640]{2,1,0:T(8,128)(2,1)}, f32[256,640]{1,0:T(8,128)}, f32[256,640]{1,0:T(8,128)}) custom-call(bf16[4,256,640]{2,1,0:T(8,128)(2,1)} %bitcast.45, bf16[256,640]{1,0:T(8,128)(2,1)} %refs_1_.3, f32[4,640]{1,0:T(4,128)} %refs_3_.5), custom_call_target="tpu_custom_call" | custom-call | tf_op jit(solution)/shard_map/pallas_call | solution.py:111
  90.1 3.6 %fusion.16 = f32[1024,1024]{0,1:T(8,128)S(1)} fusion(bf16[1024,640]{1,0:T(8,128)(2,1)} %bitcast.71, bf16[640,2560]{1,0:T(8,128)(2,1)} %bitcast.54), kind=kOutput, calls=%fused_computation.45 | convolution fusion | flops 1342177280 | bytes 6815744 | tf_op jit(solution)/shard_map/dot_general | solution.py:57
  94.4 1.0 copy-done.11
  95.4 3.2 %convolution_convert_fusion.4 = bf16[1024,640]{1,0:T(8,128)(2,1)} fusion(bf16[1024,512]{0,1:T(8,128)(2,1)S(1)} %multiply_convert_fusion.2, bf16[640,2560]{1,0:T(8,128)(2,1)} %bitcast.55), kind=kOutput, calls=%fused_computation.28 | convolution fusion | flops 671744000 | bytes 3014656 | tf_op jit(solution)/shard_map/dot_general | solution.py:61
  98.5 22.9 %shard_map.198 = (bf16[4,256,640]{2,1,0:T(8,128)(2,1)}, bf16[256,640]{1,0:T(8,128)(2,1)}, f32[1,640]{1,0:T(1,128)}) custom-call(bf16[4,256,640]{2,1,0:T(8,128)(2,1)} %bitcast.49, f32[256,640]{1,0:T(8,128)} %get-tuple-element.95.refs_1_, bf16[256,640]{1,0:T(8,128)(2,1)} %refs_3_.4, f32[4,640]{1,0:T(4,128)} %refs_3_.5), custom_call_target="tpu_custom_call" | custom-call | tf_op jit(solution)/shard_map/pallas_call | solution.py:111
  121.5 3.8 %fusion.6 = (bf16[1024,512]{0,1:T(8,128)(2,1)S(1)}, bf16[1024,512]{0,1:T(8,128)(2,1)S(1)}) fusion(f32[1024,1024]{0,1:T(8,128)S(1)} %fusion.16, bf16[1024,640]{1,0:T(8,128)(2,1)} %bitcast.73, bf16[640,2560]{1,0:T(8,128)(2,1)} %bitcast.56), kind=kOutput, calls=%fused_computation.8 | convolution fusion | flops 683671552 | bytes 8257536 | tf_op jit(solution)/shard_map/dot_general | solution.py:57
  125.3 5.2 %convolution_convert_fusion.3 = bf16[1024,640]{1,0:T(8,128)(2,1)} fusion(bf16[1024,512]{0,1:T(8,128)(2,1)S(1)} %get-tuple-element.137, bf16[1024,512]{0,1:T(8,128)(2,1)S(1)} %get-tuple-element.136, bf16[640,2560]{1,0:T(8,128)(2,1)} %bitcast.57), kind=kOutput, calls=%fused_computation.27 | convolution fusion | flops 1347026944 | bytes 4718592 | tf_op jit(solution)/shard_map/dot_general | solution.py:61
  130.6 23.0 %shard_map.199 = (bf16[4,256,640]{2,1,0:T(8,128)(2,1)}, f32[256,640]{1,0:T(8,128)}, f32[1,640]{1,0:T(1,128)}, f32[1,640]{1,0:T(1,128)}) custom-call(bf16[4,256,640]{2,1,0:T(8,128)(2,1)} %bitcast.47, f32[256,640]{1,0:T(8,128)} %get-tuple-element.95.refs_1_, f32[256,640]{1,0:T(8,128)} %get-tuple-element.98.refs_2_, bf16[256,640]{1,0:T(8,128)(2,1)} %refs_3_.4, ...), custom_call_target="tpu_custom_call" | custom-call | tf_op jit(solution)/shard_map/pallas_call | solution.py:111
  153.5 2.8 %convolution_convert_fusion.8 = bf16[640,256]{0,1:T(8,128)(2,1)} fusion(bf16[1024,640]{1,0:T(8,128)(2,1)} %bitcast.75, bf16[512,256]{1,0:T(8,128)(2,1)S(1)} %convolution_convert_fusion.9, bf16[512,256]{1,0:T(8,128)(2,1)S(1)} %convolution_convert_fusion.10), kind=kOutput, calls=%fused_computation.41 | convolution fusion | flops 336756736 | bytes 2162688 | tf_op jit(solution)/shard_map/dot_general | solution.py:67
  156.3 2.3 convolution_convert_fusion.7
  158.7 1.1 copy.30
  159.9 1.6 fusion.32
  161.5 2.3 fusion.14
  164.7 1.1 copy-done.1
  169.4 2.7 %multiply_add_fusion.3 = (f32[1024,128]{0,1:T(8,128)S(1)}, f32[1024,128]{0,1:T(8,128)S(1)}, f32[1024,128]{0,1:T(8,128)S(1)}, f32[1024,128]{0,1:T(8,128)S(1)}) fusion(f32[1024,256]{0,1:T(8,128)S(1)} %maximum_multiply_fusion.1, f32[128]{0:T(128)S(1)} %multiply_power_fusion, f32[1024,256]{0,1:T(8,128)S(1)} %convolution_add_fusion), kind=kLoop, calls=%fused_computation.84 | loop fusion | flops 1966080 | bytes 4194816 | tf_op jit(solution)/shard_map/transpose(jvp())/add_any | solution.py:45
  173.3 4.1 %convolution_convert_fusion.2 = bf16[1024,640]{1,0:T(8,128)(2,1)} fusion(bf16[640,2560]{1,0:T(8,128)(2,1)} %bitcast.59, bf16[1024,256]{0,1:T(8,128)(2,1)S(1)} %fusion.14, bf16[1024,256]{0,1:T(8,128)(2,1)S(1)} %get-tuple-element.139, bf16[1024,256]{0,1:T(8,128)(2,1)S(1)} %get-tuple-element.138), kind=kOutput, calls=%fused_computation.26 | convolution fusion | flops 1012006912 | bytes 3866624 | tf_op jit(solution)/shard_map/dot_general | solution.py:61
  177.4 14.2 %shard_map.200 = (f32[256,640]{1,0:T(8,128)}, f32[1,640]{1,0:T(1,128)}) custom-call(bf16[4,256,640]{2,1,0:T(8,128)(2,1)} %bitcast.48, bf16[256,640]{1,0:T(8,128)(2,1)} %refs_1_.3, f32[256,640]{1,0:T(8,128)} %get-tuple-element.100.refs_2_, f32[4,640]{1,0:T(4,128)} %refs_3_.5), custom_call_target="tpu_custom_call" | custom-call | tf_op jit(solution)/shard_map/pallas_call | solution.py:111
  192.9 2.4 fusion.12
  195.4 1.6 fusion.11
  198.0 1.7 copy-done.6
  199.7 51.5 %shard_map.201 = (f32[80,2688]{1,0:T(8,128)}, f32[80,256]{1,0:T(8,128)}) custom-call(bf16[8,80,2688]{2,1,0:T(8,128)(2,1)} %bitcast.46), custom_call_target="tpu_custom_call" | custom-call | tf_op jit(solution)/shard_map/pallas_call | solution.py:111
  253.5 1.4 slice.204
  255.6 1.6 slice_bitcast_fusion.1
  257.2 1.9 slice_bitcast_fusion
  (122 shorter events, 22.7 us)
Async XLA Ops:
  57.5 6.3 %copy-start.4 = (bf16[1024,768]{0,1:T(8,128)(2,1)}, bf16[1024,768]{0,1:T(8,128)(2,1)S(1)}, u32[]{:S(2)}) copy-start(bf16[1024,768]{0,1:T(8,128)(2,1)S(1)} %get-tuple-element.167) | copy-start | bytes 4718596
  60.7 1.9 copy-start.13
  60.7 1.9 copy-start.15
  60.8 1.8 copy-start.8
  61.2 1.0 copy-start.2
  63.3 1.4 copy-start
  121.5 3.8 %copy-start.27 = (f32[1,640]{1,0:T(1,128)S(1)}, f32[1,640]{1,0:T(1,128)}, u32[]{:S(2)}) copy-start(f32[1,640]{1,0:T(1,128)} %get-tuple-element.105) | copy-start | bytes 7684
  125.3 5.3 %copy-start.31 = (bf16[1024,512]{0,1:T(8,128)(2,1)}, bf16[1024,512]{0,1:T(8,128)(2,1)S(1)}, u32[]{:S(2)}) copy-start(bf16[1024,512]{0,1:T(8,128)(2,1)S(1)} %get-tuple-element.136) | copy-start | bytes 3145732
  125.3 5.2 %copy-start.33 = (bf16[1024,512]{0,1:T(8,128)(2,1)}, bf16[1024,512]{0,1:T(8,128)(2,1)S(1)}, u32[]{:S(2)}) copy-start(bf16[1024,512]{0,1:T(8,128)(2,1)S(1)} %get-tuple-element.137) | copy-start | bytes 3145732
  153.5 2.8 %copy-start.30 = (bf16[4,256,640]{2,1,0:T(8,128)(2,1)S(1)}, bf16[4,256,640]{2,1,0:T(8,128)(2,1)}, u32[]{:S(2)}) copy-start(bf16[4,256,640]{2,1,0:T(8,128)(2,1)} %get-tuple-element.99) | copy-start | bytes 3932164
  156.3 3.5 %copy-start.26 = (f32[1,640]{1,0:T(1,128)S(1)}, f32[1,640]{1,0:T(1,128)}, u32[]{:S(2)}) copy-start(f32[1,640]{1,0:T(1,128)} %get-tuple-element.103) | copy-start | bytes 7684
  156.3 3.5 %copy-start.25 = (f32[1,640]{1,0:T(1,128)S(1)}, f32[1,640]{1,0:T(1,128)}, u32[]{:S(2)}) copy-start(f32[1,640]{1,0:T(1,128)} %get-tuple-element.104) | copy-start | bytes 7684
  161.5 2.4 copy-start.3
  161.5 2.4 copy-start.5
  161.5 2.5 copy-start.7
  164.0 9.2 %copy-start.22 = (bf16[1024,256]{0,1:T(8,128)(2,1)}, bf16[1024,256]{0,1:T(8,128)(2,1)S(1)}, u32[]{:S(2)}) copy-start(bf16[1024,256]{0,1:T(8,128)(2,1)S(1)} %fusion.14) | copy-start | bytes 1572868
  164.0 1.8 copy-start.1
  166.4 1.0 copy-start.16
  167.5 1.0 copy-start.9
  173.3 4.1 %copy-start.18 = (bf16[1024,256]{0,1:T(8,128)(2,1)}, bf16[1024,256]{0,1:T(8,128)(2,1)S(1)}, u32[]{:S(2)}) copy-start(bf16[1024,256]{0,1:T(8,128)(2,1)S(1)} %get-tuple-element.138) | copy-start | bytes 1572868
  173.3 4.1 %copy-start.20 = (bf16[1024,256]{0,1:T(8,128)(2,1)}, bf16[1024,256]{0,1:T(8,128)(2,1)S(1)}, u32[]{:S(2)}) copy-start(bf16[1024,256]{0,1:T(8,128)(2,1)S(1)} %get-tuple-element.139) | copy-start | bytes 1572868
  177.4 15.4 %copy-start.10 = (bf16[4,256,640]{2,1,0:T(8,128)(2,1)S(1)}, bf16[4,256,640]{2,1,0:T(8,128)(2,1)}, u32[]{:S(2)}) copy-start(bf16[4,256,640]{2,1,0:T(8,128)(2,1)} %get-tuple-element.92) | copy-start | bytes 3932164
  177.4 15.4 %copy-start.19 = (bf16[1024,256]{0,1:T(8,128)(2,1)S(1)}, bf16[1024,256]{0,1:T(8,128)(2,1)}, u32[]{:S(2)}) copy-start(bf16[1024,256]{0,1:T(8,128)(2,1)} %copy-done.18) | copy-start | bytes 1572868
  177.4 15.4 %copy-start.21 = (bf16[1024,256]{0,1:T(8,128)(2,1)S(1)}, bf16[1024,256]{0,1:T(8,128)(2,1)}, u32[]{:S(2)}) copy-start(bf16[1024,256]{0,1:T(8,128)(2,1)} %copy-done.20) | copy-start | bytes 1572868
  192.8 2.5 copy-start.28
  192.8 2.5 copy-start.32
  192.8 2.5 copy-start.34
  195.3 1.6 copy-start.12
  195.4 1.6 copy-start.29
  198.0 1.7 copy-start.6
  199.7 59.4 %copy-start.24 = (bf16[256,640]{1,0:T(8,128)(2,1)S(1)}, bf16[256,640]{1,0:T(8,128)(2,1)}, u32[]{:S(2)}) copy-start(bf16[256,640]{1,0:T(8,128)(2,1)} %get-tuple-element.185) | copy-start | bytes 983044
  199.7 60.1 %copy-start.17 = (f32[256,640]{1,0:T(8,128)S(1)}, f32[256,640]{1,0:T(8,128)}, u32[]{:S(2)}) copy-start(f32[256,640]{1,0:T(8,128)} %get-tuple-element.186) | copy-start | bytes 1966084
  (3 other events, 2.7 us)
